TPU v7x, 32 devices: a whole 2x2x4 slice. The times are simulated.
32 devices in a mesh: group: 2 (over y), cache: 4 (over z), tensor: 2 (over x), kvsplit: 2 (over core).
Axes of the slice: x: 2, y: 2, z: 4, core: 2. Of those that a mesh axis runs over, the one named last changes fastest.
Arguments:
- cache_kv: bfloat16 [32, 256, 4, 2, 128], P(('group', 'cache'), 'kvsplit', 'tensor'), parts along dimension 0, may hold values from -6 to 6
- passage_slot: int32 [32], P('group'), parts along dimension 0, may hold values from 0 to 15, as said below
- retrieval: int32 [8, 16], P(('group', 'cache')), parts along dimension 0, may hold values from 0 to 15, as said below
- recompute: int32 [8, 256], P(('group', 'cache')), parts along dimension 0, may hold values from 0 to 4095, as said below
- new_q: bfloat16 [8, 384, 32, 128], P(('group', 'cache'), None, 'tensor'), parts along dimension 0, may hold values from -10 to 10
- new_kv: bfloat16 [8, 384, 4, 2, 128], P(('group', 'cache'), 'kvsplit', 'tensor'), parts along dimension 0, may hold values from -6 to 6
Outputs:
- attended: bfloat16 [8, 384, 4096], P(('group', 'cache'), 'kvsplit', 'tensor'), parts along dimension 0
There are 2 independent parts, one for each index of `group`. A program takes and returns all parts, laid end to end along the dimension named above; each array names one. Nothing has to cross between parts.
Inputs may be any that keep to these rules, and one draw needn't show every extreme that they name: `passage_slot`: each slot once. `retrieval`: among the 16 retrieved passages of the 1 request of one index of cache, at most 8 are stored on any one owner, and on every such index some owner stores exactly 8 of them. `recompute`: distinct and rising within a request.
All inputs are finite; a program needn't handle non-finite values.
Results may differ from a plain program's by a relative error of at most 0.0055.
Values may be sent and summed in bfloat16 or wider, within the bound.
A program may use at most 64 MiB of HBM per device.

v0:
```python
import functools
import math

import jax
import jax.numpy as jnp
from jax import lax
from jax.experimental import pallas as pl
from jax.experimental.pallas import tpu as pltpu
from jax.sharding import PartitionSpec as P

MASKED = -1e30


def attend(q_ref, keys, values, bias, acc_ref, max_ref, first, score_scale, pair):
    heads, rows, head_dim = q_ref.shape
    kv_local = keys.shape[0]
    pairs = heads // pair

    def turn(i, carry):
        at = pl.ds(i * pair, pair)
        kv = i // (pairs // kv_local)
        query = q_ref[at].reshape(pair * rows, head_dim)
        scores = lax.dot_general(
            query, keys[kv], (((1,), (1,)), ((), ())), preferred_element_type=jnp.float32
        )
        scores = scores.reshape(pair, rows, -1) * score_scale + bias[...][None]
        block_max = jnp.max(scores, axis=2, keepdims=True)
        if first:
            row_max = jnp.broadcast_to(block_max, (pair, rows, head_dim))
        else:
            former = max_ref[at]
            row_max = jnp.maximum(former, block_max)
        weights = jnp.exp2(scores - row_max[:, :, :1]).astype(jnp.bfloat16)
        part = jnp.dot(
            weights.reshape(pair * rows, -1), values[kv], preferred_element_type=jnp.float32
        ).reshape(pair, rows, 2 * head_dim)
        if first:
            acc_ref[at] = part
        else:
            shrink = jnp.exp2(former - row_max)
            acc_ref[at] = acc_ref[at] * jnp.concatenate([shrink, shrink], axis=2) + part
        max_ref[at] = row_max
        return carry

    lax.fori_loop(0, pairs, turn, 0, unroll=2)


def kernel(score_scale, pair, q_ref, fresh_ref, corpus_ref, fresh_bias, bias_ref, out_ref,
           acc_ref, max_ref, key_ref, value_ref, fresh_value):
    step = pl.program_id(0)
    heads, rows, head_dim = q_ref.shape
    kv_local = fresh_ref.shape[0]
    half = corpus_ref.shape[4]

    @pl.when(step == 0)
    def _():
        value_ref[...] = jnp.ones_like(value_ref)
        fresh_value[...] = jnp.ones_like(fresh_value)
        fresh_value[:, :, :head_dim] = fresh_ref[:, 1]
        attend(q_ref, fresh_ref.at[:, 0], fresh_value, fresh_bias, acc_ref, max_ref, True,
               score_scale, pair)

    for part in range(2):
        at = pl.ds(part * half, half)
        key_ref[:, at, :] = corpus_ref[0, part, :, 0]
        value_ref[:, at, :head_dim] = corpus_ref[0, part, :, 1]
    attend(q_ref, key_ref, value_ref, bias_ref.at[0], acc_ref, max_ref, False, score_scale, pair)

    @pl.when(step == pl.num_programs(0) - 1)
    def _():
        for head in range(heads):
            total = acc_ref[head]
            out_ref[:, head * head_dim:(head + 1) * head_dim] = (
                total[:, :head_dim] / total[:, head_dim:]
            ).astype(out_ref.dtype)


def on_device(cache_kv, passage_slot, retrieval, recompute, new_q, new_kv):
    slots, half_len, kv_local, _, head_dim = cache_kv.shape
    npass = retrieval.shape[1]
    new_rows, heads = new_q.shape[1:3]
    rc_rows = recompute.shape[1]
    owners = lax.axis_size("cache")
    holders = lax.axis_size("kvsplit")
    half_index = lax.axis_index("kvsplit")
    plen = half_len * holders
    ctx = npass * plen
    rows = new_rows // holders

    own = cache_kv.transpose(2, 3, 0, 1, 4).reshape(kv_local, 2, slots * half_len, head_dim)
    corpus = lax.all_gather(own, "cache", axis=0)
    corpus = lax.all_gather(corpus, "kvsplit", axis=1)
    fresh = lax.all_gather(new_kv[0].transpose(1, 2, 0, 3), "kvsplit", axis=2, tiled=True)

    passages = jnp.arange(passage_slot.shape[0], dtype=jnp.int32)
    chosen = jnp.sum(
        jnp.where(retrieval[0][:, None] == passages[None, :], passage_slot[None, :], 0), axis=1
    )
    question = ctx + jnp.arange(new_rows - rc_rows, dtype=jnp.int32)
    row_pos = jnp.concatenate([recompute[0], question])
    row_pos = lax.dynamic_slice_in_dim(row_pos, half_index * rows, rows, 0)
    row_pass, row_off = row_pos // plen, row_pos % plen
    context = jnp.arange(ctx, dtype=jnp.int32)
    live = jnp.logical_not(jnp.any(context[:, None] == recompute[0][None, :], axis=1))
    live = live.reshape(npass, holders, half_len).astype(jnp.bfloat16)
    entry = jnp.arange(npass, dtype=jnp.int32)
    before = (entry[None, :] < row_pass[:, None]).astype(jnp.bfloat16)
    within = (entry[None, :] == row_pass[:, None])
    row_slot = jnp.sum(jnp.where(within, chosen[None, :] + 1, 0), axis=1) - 1
    slot = jnp.arange(owners * slots, dtype=jnp.int32).reshape(owners, slots)
    held = (chosen[:, None, None] == slot[None]).astype(jnp.bfloat16)
    stored = held[:, :, None, :, None] * live[:, None, :, None, :]
    keys = holders * slots * half_len
    count = jnp.einsum("rj,jok->ork", before, stored.reshape(npass, owners, keys),
                       preferred_element_type=jnp.float32)
    edge = jnp.einsum("rj,jht->rht", within.astype(jnp.bfloat16), live,
                      preferred_element_type=jnp.float32)
    token = jnp.arange(plen, dtype=jnp.int32).reshape(holders, half_len)
    edge = jnp.where(token[None] <= row_off[:, None, None], edge, 0.0)
    mine = row_slot[None, :, None] == slot[:, None, :]
    extra = jnp.where(mine[:, :, None, :, None], edge[None, :, :, None, :], 0.0)
    count = count + extra.reshape(owners, rows, keys)
    bias = jnp.where(count > 0.5, jnp.log2(jnp.maximum(count, 1.0)), MASKED)
    new_index = jnp.arange(new_rows, dtype=jnp.int32)
    row_index = half_index * rows + jnp.arange(rows, dtype=jnp.int32)
    fresh_bias = jnp.where(new_index[None, :] <= row_index[:, None], 0.0, MASKED)

    queries = lax.dynamic_slice_in_dim(new_q[0], half_index * rows, rows, 0).transpose(1, 0, 2)
    score_scale = head_dim ** (-0.5) * math.log2(math.e)
    whole = lambda *shape: pl.BlockSpec(shape, lambda i: (0,) * len(shape))
    result = pl.pallas_call(
        functools.partial(kernel, score_scale, 2),
        grid=(owners,),
        out_shape=jax.ShapeDtypeStruct((rows, heads * head_dim), jnp.bfloat16),
        in_specs=[
            whole(heads, rows, head_dim),
            whole(kv_local, 2, new_rows, head_dim),
            pl.BlockSpec((1, holders, kv_local, 2, slots * half_len, head_dim),
                         lambda i: (i, 0, 0, 0, 0, 0)),
            whole(rows, new_rows),
            pl.BlockSpec((1, rows, keys), lambda i: (i, 0, 0)),
        ],
        out_specs=whole(rows, heads * head_dim),
        scratch_shapes=[
            pltpu.VMEM((heads, rows, 2 * head_dim), jnp.float32),
            pltpu.VMEM((heads, rows, head_dim), jnp.float32),
            pltpu.VMEM((kv_local, keys, head_dim), jnp.bfloat16),
            pltpu.VMEM((kv_local, keys, 2 * head_dim), jnp.bfloat16),
            pltpu.VMEM((kv_local, new_rows, 2 * head_dim), jnp.bfloat16),
        ],
        compiler_params=pltpu.CompilerParams(vmem_limit_bytes=48 * 1024 * 1024),
    )(queries, fresh, corpus, fresh_bias, bias)
    return result[None]


def solution(mesh):
    in_specs = (
        P(("group", "cache"), "kvsplit", "tensor", None, None),
        P("group"),
        P(("group", "cache"), None),
        P(("group", "cache"), None),
        P(("group", "cache"), None, "tensor", None),
        P(("group", "cache"), "kvsplit", "tensor", None, None),
    )
    out_specs = P(("group", "cache"), "kvsplit", "tensor")
    return jax.shard_map(
        on_device, mesh=mesh, in_specs=in_specs, out_specs=out_specs, check_vma=False
    )
```

profile of v0, /device:TPU:0, one launch (start us, length us, event | category | flops | bytes accessed | tf_op | source)
XLA Modules:
  0.0 115.6 jit_solution(15923229275240463589)
XLA Ops:
  6.5 0.0 copy-start
  6.5 0.0 copy-start.4
  6.5 0.0 copy-start.6
  6.5 0.0 copy-start.5
  6.5 0.0 copy-start.3
  6.5 0.0 all-gather.4.cloned.1.call-start
  6.6 2.1 %copy.24 = bf16[2,2,4,128,128]{4,3,2,1,0:T(8,128)(2,1)} copy(bf16[2,2,4,128,128]{4,1,0,3,2:T(2,128)(2,1)} %bitcast.32) | data formatting | bytes 1048576 | tf_op jit(solution)/shard_map/transpose | solution.py:90
  8.6 0.0 all-gather.4.cloned.1.call-update
  8.7 0.0 all-gather.6.cloned.1.call-start
  8.7 48.9 %all-gather.4.cloned.1.call-done = bf16[4,2,2,512,128]{4,3,2,1,0:T(8,128)(2,1)} async-done(((bf16[1,2,2,512,128]{4,3,2,1,0:T(8,128)(2,1)}), bf16[4,2,2,512,128]{4,3,2,1,0:T(8,128)(2,1)}) %all-gather.4.cloned.1.call-update) | async-done | bytes 2097168 | tf_op jit(solution)/shard_map/all_gather | solution.py:91
  57.6 0.0 all-gather.6.cloned.1.call-update
  57.7 0.0 copy-done.4
  57.7 0.6 fusion
  58.4 0.0 copy-done.6
  58.4 0.0 copy-done.5
  58.4 0.2 select_reduce_fusion.1
  58.6 0.1 compare_convert_fusion
  58.7 0.1 mul.26
  58.8 0.1 mul.27
  58.9 0.1 and_select_fusion
  59.0 0.2 convolution_select_fusion
  59.3 0.2 copy.26
  59.4 0.0 copy-done.3
  59.5 0.1 broadcast_in_dim.95
  59.6 1.2 %broadcast_in_dim.96 = f32[192,1024]{1,0:T(8,128)} reshape(f32[192,2,4,128]{3,2,1,0:T(4,128)S(1)} %broadcast_in_dim.95) | data formatting | bytes 1572864 | tf_op jit(solution)/shard_map/jit(_where)/broadcast_in_dim | solution.py:121
  60.8 0.1 select_reduce_fusion
  60.9 0.1 broadcast_compare_fusion
  61.0 1.1 broadcast_in_dim.92
  62.2 2.1 %broadcast_in_dim.93 = pred[4,192,1024]{2,1,0:T(32,128)(4,1)} reshape(pred[4,192,2,4,128]{4,3,2,1,0:T(4,128)(4,1)S(1)} %broadcast_in_dim.92) | data formatting | bytes 1572864 | tf_op jit(solution)/shard_map/jit(_where)/broadcast_in_dim | solution.py:121
  64.3 0.0 copy-done
  64.3 0.0 copy-start.2
  64.3 0.1 constant_dynamic-slice_fusion
  64.5 0.2 copy.31
  64.7 2.1 %all_gather.12.fresh_ref = bf16[2,2,384,128]{3,2,1,0:T(8,128)(2,1)S(1)} all-gather(bf16[2,2,192,128]{3,2,1,0:T(8,128)(2,1)S(1)} %bitcast.31), channel_id=1, replica_groups=mesh['group'=2,'cache'=4,'tensor'=2,'kvsplit'=2] {'kvsplit'}, dimensions={2}, use_global_device_ids=true | all-gather | bytes 589824 | tf_op jit(solution)/shard_map/all_gather | solution.py:93
  66.8 0.1 fusion.1.fresh_bias
  66.9 0.0 copy-done.2
  66.9 4.2 %multiply_select_fusion.bias_ref = f32[4,192,1024]{2,1,0:T(8,128)} fusion(pred[4,192,1024]{2,1,0:T(32,128)(4,1)S(1)} %copy-done.2, f32[192,1024]{1,0:T(8,128)} %broadcast_in_dim.96, bf16[16,4,1024]{2,0,1:T(8,128)(2,1)S(1)} %mul.27, bf16[16,1024]{1,0:T(8,128)(2,1)S(1)} %mul.29, s32[192]{0:T(256)S(1)} %get-tuple-element.6), kind=kOutput, calls=%fused_computation.3 | convolution fusion | flops 29953024 | bytes 4883200 | tf_op jit(solution)/shard_map/rj,jok->ork/dot_general | solution.py:114
  71.1 0.5 all-gather.6.cloned.1.call-done
  71.6 0.0 copy-start.1
  71.6 1.9 %copy-done.1 = f32[4,192,1024]{2,1,0:T(8,128)S(1)} copy-done((f32[4,192,1024]{2,1,0:T(8,128)S(1)}, f32[4,192,1024]{2,1,0:T(8,128)}, u32[]{:S(2)}) %copy-start.1) | copy-done | bytes 3145752
  73.5 35.3 %shard_map.64 = bf16[192,2048]{1,0:T(8,128)(2,1)} custom-call(bf16[16,192,128]{2,1,0:T(8,128)(2,1)S(1)} %bitcast.28, bf16[2,2,384,128]{3,2,1,0:T(8,128)(2,1)S(1)} %all_gather.12.fresh_ref, bf16[4,2,2,2,512,128]{5,4,3,2,1,0:T(8,128)(2,1)} %bitcast.29, f32[192,384]{1,0:T(8,128)S(1)} %fusion.1.fresh_bias, f32[4,192,1024]{2,1,0:T(8,128)S(1)} %copy-done.1), custom_call_target="tpu_custom_call" | custom-call | tf_op jit(solution)/shard_map/pallas_call | solution.py:131
  (13 shorter events, 0.1 us)
Async XLA Ops:
  6.5 57.8 %copy-start = (bf16[1,384,16,128]{3,2,1,0:T(8,128)(2,1)S(1)}, bf16[1,384,16,128]{3,2,1,0:T(8,128)(2,1)}, u32[]{:S(2)}) copy-start(bf16[1,384,16,128]{3,2,1,0:T(8,128)(2,1)} %param.10) | copy-start | bytes 4718596
  6.5 51.1 %copy-start.4 = (s32[1,256]{1,0:T(1,128)S(1)}, s32[1,256]{1,0:T(1,128)}, u32[]{:S(2)}) copy-start(s32[1,256]{1,0:T(1,128)} %param.9) | copy-start | bytes 3076
  6.5 51.9 %copy-start.6 = (s32[1,16]{1,0:T(1,128)S(1)}, s32[1,16]{1,0:T(1,128)}, u32[]{:S(2)}) copy-start(s32[1,16]{1,0:T(1,128)} %param.8) | copy-start | bytes 196
  6.5 51.9 %copy-start.5 = (s32[16]{0:T(128)S(1)}, s32[16]{0:T(128)}, u32[]{:S(2)}) copy-start(s32[16]{0:T(128)} %param.7) | copy-start | bytes 196
  6.5 52.9 %copy-start.3 = (bf16[1,192,2,2,128]{4,3,2,1,0:T(2,128)(2,1)S(1)}, bf16[1,192,2,2,128]{4,3,2,1,0:T(2,128)(2,1)}, u32[]{:S(2)}) copy-start(bf16[1,192,2,2,128]{4,3,2,1,0:T(2,128)(2,1)} %param.11) | copy-start | bytes 589828
  6.5 51.1 %all-gather.4.cloned.1.call-start = ((), (), s32[]{:S(2)}) async-start(), calls=%async_computation | async-start | bytes 2621440 | tf_op jit(solution)/shard_map/all_gather | solution.py:91
  8.7 62.9 %all-gather.6.cloned.1.call-start = ((), (), s32[]{:S(2)}) async-start(), calls=%async_computation.1 | async-start | bytes 6291456 | tf_op jit(solution)/shard_map/all_gather | solution.py:92
  64.3 2.5 %copy-start.2 = (pred[4,192,1024]{2,1,0:T(32,128)(4,1)S(1)}, pred[4,192,1024]{2,1,0:T(32,128)(4,1)}, u32[]{:S(2)}) copy-start(pred[4,192,1024]{2,1,0:T(32,128)(4,1)} %broadcast_in_dim.93) | copy-start | bytes 2359300
  71.6 1.9 %copy-start.1 = (f32[4,192,1024]{2,1,0:T(8,128)S(1)}, f32[4,192,1024]{2,1,0:T(8,128)}, u32[]{:S(2)}) copy-start(f32[4,192,1024]{2,1,0:T(8,128)} %multiply_select_fusion.bias_ref) | copy-start | bytes 9437188
Sparse Core Ops, SparseCore 0:
  9.0 48.6 all-gather.3
  59.2 12.3 all-gather.5
where the time goes:
time: 116 us
  waiting for transfers between devices  49.4 us (43%)
  Pallas kernels  35.3 us (30%)
  between operations  13.6 us (12%)
  local copies, waits for them, and re-layouts  9.34 us (8%)
  matrix products  4.49 us (4%)
  blocking collectives  2.09 us (2%)
  other arithmetic  1.33 us (1%)
    all_gather x1, waiting for transfers between devices, on_device(): corpus = lax.all_gather(own, 'cache', axis=0)  48.9 us
    pallas_call x1, Pallas kernels, on_device(): pl.pallas_call(functools.partial(kernel, score_scale, 2), grid=(owners,),...  35.3 us
    broadcast_in_dim x4, local copies, waits for them, and re-layouts, on_device(): extra = jnp.where(mine[:, :, None, :, None], edge[None, :, :, None, :], 0.0)  4.6 us
    dot_general x1, matrix products, on_device(): jnp.einsum('rj,jok->ork', before, stored.reshape(npass, owners, keys), pr...  4.25 us
  transfers between devices with their start and end apart: 2, of which 2 were waited for; matrix products, arithmetic and copies ran while one was open for 10% of the time, Pallas kernels for 0%

commit v1 on v0

v1 whole, which is shorter than its diff:
```python
import functools
import math

import jax
import jax.numpy as jnp
from jax import lax
from jax.experimental import pallas as pl
from jax.experimental.pallas import tpu as pltpu
from jax.sharding import PartitionSpec as P

MASKED = -1e30


MESH = pl.DeviceIdType.MESH


def attend(q_ref, kv, keys, value_ref, bias_ref, acc_ref, max_ref, first, score_scale, pair):
    heads, rows, head_dim = q_ref.shape
    group = heads // keys[1]
    pairs = group // pair

    def turn(i, carry):
        at = pl.ds(kv * group + i * pair, pair)
        query = q_ref[at].reshape(pair * rows, head_dim)
        scores = lax.dot_general(
            query, keys[0](), (((1,), (1,)), ((), ())), preferred_element_type=jnp.float32
        )
        scores = scores.reshape(pair, rows, -1) * score_scale + bias_ref[...][None]
        block_max = jnp.max(scores, axis=2, keepdims=True)
        if first:
            row_max = jnp.broadcast_to(block_max, (pair, rows, head_dim))
        else:
            former = max_ref[at]
            row_max = jnp.maximum(former, block_max)
        weights = jnp.exp2(scores - row_max[:, :, :1]).astype(jnp.bfloat16)
        part = jnp.dot(
            weights.reshape(pair * rows, -1), value_ref[...], preferred_element_type=jnp.float32
        ).reshape(pair, rows, 2 * head_dim)
        if first:
            acc_ref[at] = part
        else:
            shrink = jnp.exp2(former - row_max)
            acc_ref[at] = acc_ref[at] * jnp.concatenate([shrink, shrink], axis=2) + part
        max_ref[at] = row_max
        return carry

    lax.fori_loop(0, pairs, turn, 0, unroll=2)


def kernel(score_scale, pair, owners, q_ref, fresh_ref, own_ref, stored_ref, live_ref, before_ref,
           within_ref, slot_ref, offset_ref, out_ref,
           acc_ref, max_ref, value_ref, new_value_ref, bias_ref, new_bias_ref, edge_ref,
           corpus_ref, new_ref, line_send, line_recv, side_send, side_recv, new_send, new_recv):
    heads, rows, head_dim = q_ref.shape
    kv_local, _, half, _ = own_ref.shape
    new_half = fresh_ref.shape[2]
    plen = live_ref.shape[1]
    half_len = plen // 2
    slots = half // half_len
    z = lax.axis_index("cache")
    mine = lax.axis_index("kvsplit")
    other = 1 - mine
    has_left, has_right = z > 0, z < owners - 1

    barrier = pltpu.get_barrier_semaphore()
    pl.semaphore_signal(barrier, inc=1, device_id={"kvsplit": other}, device_id_type=MESH)

    @pl.when(has_left)
    def _():
        pl.semaphore_signal(barrier, inc=1, device_id={"cache": z - 1}, device_id_type=MESH)

    @pl.when(has_right)
    def _():
        pl.semaphore_signal(barrier, inc=1, device_id={"cache": z + 1}, device_id_type=MESH)

    peers = 1 + jnp.minimum(z, 1) + jnp.minimum(owners - 1 - z, 1)
    pl.semaphore_wait(barrier, peers)

    def line_copy(block, owner, kv, way):
        return pltpu.make_async_remote_copy(
            src_ref=block, dst_ref=corpus_ref.at[owner, mine, kv],
            send_sem=line_send.at[way, owner, kv], recv_sem=line_recv.at[owner, kv],
            device_id={"cache": z + 1 if way else z - 1}, device_id_type=MESH)

    def side_copy(block, owner, kv):
        return pltpu.make_async_remote_copy(
            src_ref=block, dst_ref=corpus_ref.at[owner, mine, kv],
            send_sem=side_send.at[owner, kv], recv_sem=side_recv.at[owner, kv],
            device_id={"kvsplit": other}, device_id_type=MESH)

    new_copy = pltpu.make_async_remote_copy(
        src_ref=fresh_ref, dst_ref=new_ref.at[mine], send_sem=new_send, recv_sem=new_recv,
        device_id={"kvsplit": other}, device_id_type=MESH)

    for kv in range(kv_local):
        @pl.when(has_left)
        def _():
            line_copy(own_ref.at[kv], z, kv, 0).start()

        @pl.when(has_right)
        def _():
            line_copy(own_ref.at[kv], z, kv, 1).start()

    new_copy.start()
    for kv in range(kv_local):
        side_copy(own_ref.at[kv], z, kv).start()

    near = jnp.minimum(z, owners - 1 - z)

    def source(k):
        both = k < 2 * near
        far = jnp.where(both, k // 2 + 1, k - near + 1)
        left = jnp.where(both, k % 2, jnp.where(z > owners - 1 - z, 0, 1)) == 0
        return jnp.where(left, z - far, z + far), left

    def arrive(k, kv):
        owner, left = source(k)
        block = corpus_ref.at[owner, mine, kv]
        side = side_copy(block, owner, kv)
        line_copy(block, owner, kv, 1).wait_recv()

        @pl.when(jnp.logical_and(left, has_right))
        def _():
            line_copy(block, owner, kv, 1).start()

        @pl.when(jnp.logical_and(jnp.logical_not(left), has_left))
        def _():
            line_copy(block, owner, kv, 0).start()

        side.start()

    def compute(owner, kv):
        side_copy(corpus_ref.at[owner, mine, kv], owner, kv).wait_recv()
        if kv == 0:
            count = jnp.dot(before_ref[...], stored_ref[owner],
                            preferred_element_type=jnp.float32)
            for h in range(2):
                edge = edge_ref[:, h * half_len:(h + 1) * half_len]
                for s in range(slots):
                    at = slice((h * slots + s) * half_len, (h * slots + s + 1) * half_len)
                    total = count[:, at] + jnp.where(
                        slot_ref[...] == owner * slots + s, edge, 0.0)
                    bias_ref[:, at] = jnp.where(
                        total > 0.5, jnp.log2(jnp.maximum(total, 1.0)), MASKED)
        for h in range(2):
            value_ref[h * half:(h + 1) * half, :head_dim] = corpus_ref[owner, h, kv, 1]
        keys = lambda: corpus_ref[owner, :, kv, 0].reshape(2 * half, head_dim)
        attend(q_ref, kv, (keys, kv_local), value_ref, bias_ref, acc_ref, max_ref, False,
               score_scale, pair)

    corpus_ref[z, mine] = own_ref[...]
    new_ref[mine] = fresh_ref[...]
    value_ref[:, head_dim:] = jnp.ones((2 * half, head_dim), jnp.bfloat16)
    new_value_ref[:, head_dim:] = jnp.ones((2 * new_half, head_dim), jnp.bfloat16)
    token = lax.broadcasted_iota(jnp.int32, (rows, plen), 1)
    edge_ref[...] = jnp.where(
        token <= offset_ref[...],
        jnp.dot(within_ref[...], live_ref[...], preferred_element_type=jnp.float32), 0.0)
    row = lax.broadcasted_iota(jnp.int32, (rows, 2 * new_half), 0) + mine * rows
    column = lax.broadcasted_iota(jnp.int32, (rows, 2 * new_half), 1)
    new_bias_ref[...] = jnp.where(column <= row, 0.0, MASKED)

    new_copy.wait_recv()
    for kv in range(kv_local):
        for h in range(2):
            new_value_ref[h * new_half:(h + 1) * new_half, :head_dim] = new_ref[h, kv, 1]
        keys = lambda: new_ref[:, kv, 0].reshape(2 * new_half, head_dim)
        attend(q_ref, kv, (keys, kv_local), new_value_ref, new_bias_ref, acc_ref, max_ref, True,
               score_scale, pair)

    for kv in range(kv_local - 1):
        compute(z, kv)

    def turn(k, carry):
        for kv in range(kv_local):
            arrive(k, kv)
            if kv == 0:
                compute(jnp.where(k == 0, z, source(jnp.maximum(k - 1, 0))[0]), kv_local - 1)
            else:
                compute(source(k)[0], kv - 1)
        return carry

    lax.fori_loop(0, owners - 1, turn, 0)
    compute(source(owners - 2)[0], kv_local - 1)

    for head in range(heads):
        total = acc_ref[head]
        out_ref[:, head * head_dim:(head + 1) * head_dim] = (
            total[:, :head_dim] / total[:, head_dim:]
        ).astype(out_ref.dtype)

    for kv in range(kv_local):
        @pl.when(has_left)
        def _():
            line_copy(own_ref.at[kv], z, kv, 0).wait_send()

        @pl.when(has_right)
        def _():
            line_copy(own_ref.at[kv], z, kv, 1).wait_send()

        side_copy(own_ref.at[kv], z, kv).wait_send()
    new_copy.wait_send()

    def sent(k, carry):
        owner, left = source(k)
        for kv in range(kv_local):
            block = corpus_ref.at[owner, mine, kv]

            @pl.when(jnp.logical_and(left, has_right))
            def _():
                line_copy(block, owner, kv, 1).wait_send()

            @pl.when(jnp.logical_and(jnp.logical_not(left), has_left))
            def _():
                line_copy(block, owner, kv, 0).wait_send()

            side_copy(block, owner, kv).wait_send()
        return carry

    lax.fori_loop(0, owners - 1, sent, 0)


def on_device(cache_kv, passage_slot, retrieval, recompute, new_q, new_kv):
    slots, half_len, kv_local, _, head_dim = cache_kv.shape
    npass = retrieval.shape[1]
    new_rows, heads = new_q.shape[1:3]
    rc_rows = recompute.shape[1]
    owners = lax.axis_size("cache")
    holders = lax.axis_size("kvsplit")
    half_index = lax.axis_index("kvsplit")
    plen = half_len * holders
    ctx = npass * plen
    rows = new_rows // holders

    own = cache_kv.transpose(2, 3, 0, 1, 4).reshape(kv_local, 2, slots * half_len, head_dim)
    fresh = new_kv[0].transpose(1, 2, 0, 3)

    passages = jnp.arange(passage_slot.shape[0], dtype=jnp.int32)
    chosen = jnp.sum(
        jnp.where(retrieval[0][:, None] == passages[None, :], passage_slot[None, :], 0), axis=1
    )
    question = ctx + jnp.arange(new_rows - rc_rows, dtype=jnp.int32)
    row_pos = jnp.concatenate([recompute[0], question])
    row_pos = lax.dynamic_slice_in_dim(row_pos, half_index * rows, rows, 0)
    row_pass, row_off = row_pos // plen, row_pos % plen
    context = jnp.arange(ctx, dtype=jnp.int32)
    live = jnp.logical_not(jnp.any(context[:, None] == recompute[0][None, :], axis=1))
    live = live.reshape(npass, holders, half_len).astype(jnp.bfloat16)
    entry = jnp.arange(npass, dtype=jnp.int32)
    before = (entry[None, :] < row_pass[:, None]).astype(jnp.bfloat16)
    within = (entry[None, :] == row_pass[:, None])
    row_slot = jnp.sum(jnp.where(within, chosen[None, :] + 1, 0), axis=1) - 1
    slot = jnp.arange(owners * slots, dtype=jnp.int32).reshape(owners, slots)
    keys = holders * slots * half_len
    held = (chosen[None, :, None] == slot[:, None, :]).astype(jnp.bfloat16)
    stored = held[:, :, None, :, None] * live[None, :, :, None, :]
    stored = stored.reshape(owners, npass, keys)

    queries = lax.dynamic_slice_in_dim(new_q[0], half_index * rows, rows, 0).transpose(1, 0, 2)
    score_scale = head_dim ** (-0.5) * math.log2(math.e)
    dma = pltpu.SemaphoreType.DMA
    result = pl.pallas_call(
        functools.partial(kernel, score_scale, 2, owners),
        out_shape=jax.ShapeDtypeStruct((rows, heads * head_dim), jnp.bfloat16),
        in_specs=[pl.BlockSpec(memory_space=pltpu.VMEM)] * 9,
        out_specs=pl.BlockSpec(memory_space=pltpu.VMEM),
        scratch_shapes=[
            pltpu.VMEM((heads, rows, 2 * head_dim), jnp.float32),
            pltpu.VMEM((heads, rows, head_dim), jnp.float32),
            pltpu.VMEM((keys, 2 * head_dim), jnp.bfloat16),
            pltpu.VMEM((new_rows, 2 * head_dim), jnp.bfloat16),
            pltpu.VMEM((rows, keys), jnp.float32),
            pltpu.VMEM((rows, new_rows), jnp.float32),
            pltpu.VMEM((rows, plen), jnp.float32),
            pltpu.VMEM((owners, holders) + own.shape, jnp.bfloat16),
            pltpu.VMEM((holders,) + fresh.shape, jnp.bfloat16),
            dma((2, owners, kv_local)),
            dma((owners, kv_local)),
            dma((owners, kv_local)),
            dma((owners, kv_local)),
            dma(()),
            dma(()),
        ],
        compiler_params=pltpu.CompilerParams(
            vmem_limit_bytes=56 * 1024 * 1024, collective_id=0, has_side_effects=True),
    )(queries, fresh, own, stored, live.reshape(npass, plen), before,
      within.astype(jnp.bfloat16), row_slot[:, None], row_off[:, None])
    return result[None]


def solution(mesh):
    in_specs = (
        P(("group", "cache"), "kvsplit", "tensor", None, None),
        P("group"),
        P(("group", "cache"), None),
        P(("group", "cache"), None),
        P(("group", "cache"), None, "tensor", None),
        P(("group", "cache"), "kvsplit", "tensor", None, None),
    )
    out_specs = P(("group", "cache"), "kvsplit", "tensor")
    return jax.shard_map(
        on_device, mesh=mesh, in_specs=in_specs, out_specs=out_specs, check_vma=False
    )
```

time: 116 us -> 68.3 us (0.59)
  waiting for transfers between devices: 49.4 us -> 0 us
  Pallas kernels: 35.3 us -> 55.1 us
  between operations: 13.6 us -> 0.08 us
  matrix products: 4.49 us -> 0 us
  other arithmetic: 1.33 us -> 4.73 us
  blocking collectives: 2.09 us -> 0 us
    all_gather x2 -> x0, waiting for transfers between devices: 49.4 us -> none  [the longest x1 48.9 us: on_device(): corpus = lax.all_gather(own, 'cache', axis=0)]
    pallas_call x1, Pallas kernels: 35.3 us -> 55.1 us  [on_device(): pl.pallas_call(functools.partial(kernel, score_scale, 2, owners), out_sha...]
    dot_general x2 -> x0, matrix products: 4.49 us -> none  [the longest x1 4.25 us: on_device(): jnp.einsum('rj,jok->ork', before, stored.reshape(npass, owners, keys), pr...]
    broadcast_in_dim x4 -> x1, local copies, waits for them, and re-layouts: 4.6 us -> 0.77 us  [on_device(): row_off[:, None]]
    all_gather x1 -> x0, blocking collectives: 2.09 us -> none  [on_device(): lax.all_gather(new_kv[0].transpose(1, 2, 0, 3), 'kvsplit', axis=2, tiled=...]
    unnamed x15 -> x6, local copies, waits for them, and re-layouts: 1.94 us -> 3.73 us
  transfers between devices with their start and end apart: 2 -> 0, of which waited for: 2 -> 0; matrix products, arithmetic and copies ran while one was open for 10% -> 0% of each run, Pallas kernels for 0% -> 0%
where the time goes in v1:
time: 68.3 us; the launch traced here: 68.1 us
  Pallas kernels  55.1 us (81%)
  local copies, waits for them, and re-layouts  8.22 us (12%)
  other arithmetic  4.73 us (7%)
    pallas_call x1, Pallas kernels, on_device(): pl.pallas_call(functools.partial(kernel, score_scale, 2, owners), out_sha...  55.1 us
    unnamed x6, local copies, waits for them, and re-layouts  3.73 us

profile of v1, /device:TPU:0, one launch (start us, length us, event | category | flops | bytes accessed | tf_op | source)
XLA Modules:
  0.0 68.1 jit_solution(13153050987465140161)
XLA Ops:
  0.0 0.0 copy-start
  0.0 0.0 copy-start.1
  0.0 1.0 %select_reduce_fusion.1 = s32[16]{0:T(128)S(1)} fusion(s32[16]{0:T(128)} %param.7, s32[16]{0:T(128)} %bitcast.28), kind=kLoop, calls=%fused_computation.12 | loop fusion | flops 752 | bytes 192 | tf_op jit(solution)/shard_map/reduce_sum | solution.py:239
  1.0 0.7 %pad_add_fusion = s32[384]{0:T(512)S(1)} fusion(s32[128]{0:T(128)S(1)} %iota_add_fusion, s32[256]{0:T(256)} %bitcast.26), kind=kLoop, calls=%fused_computation.14 | loop fusion | flops 384 | bytes 3072 | tf_op jit(solution)/shard_map/concatenate | solution.py:243
  1.7 0.1 and_select_fusion
  1.8 0.2 select_reduce_fusion
  2.0 1.3 %fusion = pred[4096]{0:T(1024)(128)(4,1)S(1)} fusion(s32[256]{0:T(256)} %bitcast.27), kind=kLoop, calls=%fused_computation.1 | loop fusion | flops 2093056 | bytes 5120 | tf_op jit(solution)/shard_map/reduce_or | solution.py:247
  3.3 0.6 reshape.57.live_ref
  3.9 0.1 compare_convert_fusion
  4.0 0.8 %copy.18.slot_ref = s32[192,1]{1,0:T(8,128)} copy(s32[192,1]{0,1:T(1,128)S(1)} %bitcast.25) | data formatting | bytes 1536 | tf_op jit(solution)/shard_map/sub | solution.py:252
  4.8 0.8 %copy.19.offset_ref = s32[192,1]{1,0:T(8,128)} copy(s32[192,1]{0,1:T(1,128)S(1)} %bitcast.24) | data formatting | bytes 1536 | tf_op jit(solution)/shard_map/broadcast_in_dim | solution.py:287
  5.6 0.7 %fusion.1 = (bf16[192,16]{1,0:T(8,128)(2,1)}, bf16[192,16]{1,0:T(8,128)(2,1)}) fusion(s32[192]{0:T(256)S(1)} %get-tuple-element.6), kind=kLoop, calls=%fused_computation.6 | loop fusion | flops 12288 | bytes 13056 | tf_op jit(solution)/shard_map/convert_element_type | solution.py:287
  6.3 0.1 mul.25
  6.4 0.1 mul.26
  6.5 0.7 broadcast_multiply_fusion.stored_ref
  7.2 1.6 %copy.23 = bf16[1,192,2,2,128]{4,1,3,2,0:T(8,128)(2,1)} copy(bf16[1,192,2,2,128]{4,3,2,1,0:T(2,128)(2,1)} %param.11) | data formatting | bytes 393216 | tf_op args[5]
  8.8 0.0 copy-done.1
  8.8 0.9 %copy.17 = bf16[2,2,4,128,128]{4,3,2,1,0:T(8,128)(2,1)} copy(bf16[2,2,4,128,128]{4,1,0,3,2:T(2,128)(2,1)S(1)} %bitcast.22) | data formatting | bytes 1048576 | tf_op jit(solution)/shard_map/transpose | solution.py:235
  9.7 0.0 copy-done
  9.7 0.1 constant_dynamic-slice_fusion
  9.9 1.1 %copy.22 = bf16[1,192,16,128]{3,1,2,0:T(8,128)(2,1)} copy(bf16[1,192,16,128]{3,2,1,0:T(8,128)(2,1)S(1)} %constant_dynamic-slice_fusion) | data formatting | bytes 1572864 | tf_op jit(solution)/shard_map/dynamic_slice | solution.py:259
  10.9 55.1 %shard_map.64 = bf16[192,2048]{1,0:T(8,128)(2,1)} custom-call(bf16[16,192,128]{2,1,0:T(8,128)(2,1)} %bitcast.18, bf16[2,2,192,128]{3,2,1,0:T(8,128)(2,1)} %bitcast.21, bf16[2,2,512,128]{3,2,1,0:T(8,128)(2,1)} %bitcast.20, bf16[4,16,1024]{2,1,0:T(8,128)(2,1)} %broadcast_multiply_fusion.stored_ref, bf16[16,256]{1,0:T(8,128)(2,1)} %reshape.57.live_ref, ...), custom_call_target="tpu_custom_call" | custom-call | tf_op jit(solution)/shard_map/pallas_call | solution.py:262
  66.0 2.1 %copy.25 = bf16[1,192,2048]{2,1,0:T(8,128)(2,1)} copy(bf16[1,192,2048]{2,1,0:T(8,128)(2,1)} %bitcast.19) | data formatting | bytes 1572864
  (7 shorter events, 0.1 us)
Async XLA Ops:
  0.0 9.7 %copy-start = (bf16[1,384,16,128]{3,2,1,0:T(8,128)(2,1)S(1)}, bf16[1,384,16,128]{3,2,1,0:T(8,128)(2,1)}, u32[]{:S(2)}) copy-start(bf16[1,384,16,128]{3,2,1,0:T(8,128)(2,1)} %param.10) | copy-start | bytes 4718596
  0.0 8.8 %copy-start.1 = (bf16[4,128,2,2,128]{4,3,2,1,0:T(2,128)(2,1)S(1)}, bf16[4,128,2,2,128]{4,3,2,1,0:T(2,128)(2,1)}, u32[]{:S(2)}) copy-start(bf16[4,128,2,2,128]{4,3,2,1,0:T(2,128)(2,1)} %param.6) | copy-start | bytes 1572868

commit v2 on v1

--- a/solution.py
+++ b/solution.py
@@ -19,8 +19,8 @@
     group = heads // keys[1]
     pairs = group // pair
 
-    def turn(i, carry):
-        at = pl.ds(kv * group + i * pair, pair)
+    for i in range(pairs):
+        at = slice(kv * group + i * pair, kv * group + (i + 1) * pair)
         query = q_ref[at].reshape(pair * rows, head_dim)
         scores = lax.dot_general(
             query, keys[0](), (((1,), (1,)), ((), ())), preferred_element_type=jnp.float32
@@ -42,15 +42,12 @@
             shrink = jnp.exp2(former - row_max)
             acc_ref[at] = acc_ref[at] * jnp.concatenate([shrink, shrink], axis=2) + part
         max_ref[at] = row_max
-        return carry
-
-    lax.fori_loop(0, pairs, turn, 0, unroll=2)
-
-
-def kernel(score_scale, pair, owners, q_ref, fresh_ref, own_ref, stored_ref, live_ref, before_ref,
-           within_ref, slot_ref, offset_ref, out_ref,
+
+
+def kernel(score_scale, pair, owners, q_ref, fresh_ref, own_ref, place_ref, chosen_ref, again_ref,
+           out_ref,
            acc_ref, max_ref, value_ref, new_value_ref, bias_ref, new_bias_ref, edge_ref,
-           corpus_ref, new_ref, line_send, line_recv, side_send, side_recv, new_send, new_recv):
+           live_ref, before_ref, slot_ref, entry_ref, corpus_ref, new_ref, line_send, line_recv, side_send, side_recv, new_send, new_recv):
     heads, rows, head_dim = q_ref.shape
     kv_local, _, half, _ = own_ref.shape
     new_half = fresh_ref.shape[2]
@@ -132,13 +129,15 @@
     def compute(owner, kv):
         side_copy(corpus_ref.at[owner, mine, kv], owner, kv).wait_recv()
         if kv == 0:
-            count = jnp.dot(before_ref[...], stored_ref[owner],
-                            preferred_element_type=jnp.float32)
             for h in range(2):
                 edge = edge_ref[:, h * half_len:(h + 1) * half_len]
                 for s in range(slots):
                     at = slice((h * slots + s) * half_len, (h * slots + s + 1) * half_len)
-                    total = count[:, at] + jnp.where(
+                    held = jnp.where(entry_ref[...] == owner * slots + s,
+                                     live_ref[:, h * half_len:(h + 1) * half_len], 0.0)
+                    count = jnp.dot(before_ref[...], held.astype(jnp.bfloat16),
+                                    preferred_element_type=jnp.float32)
+                    total = count + jnp.where(
                         slot_ref[...] == owner * slots + s, edge, 0.0)
                     bias_ref[:, at] = jnp.where(
                         total > 0.5, jnp.log2(jnp.maximum(total, 1.0)), MASKED)
@@ -152,10 +151,41 @@
     new_ref[mine] = fresh_ref[...]
     value_ref[:, head_dim:] = jnp.ones((2 * half, head_dim), jnp.bfloat16)
     new_value_ref[:, head_dim:] = jnp.ones((2 * new_half, head_dim), jnp.bfloat16)
-    token = lax.broadcasted_iota(jnp.int32, (rows, plen), 1)
+    npass, recomputed, stored = chosen_ref.shape[1], again_ref.shape[1], place_ref.shape[1]
+    iota = lambda shape, dim: lax.broadcasted_iota(jnp.int32, shape, dim)
+
+    def column(row, length, start):
+        shape = (length, row.shape[1])
+        return jnp.sum(jnp.where(iota(shape, 1) == iota(shape, 0) + start, row, 0),
+                       axis=1, keepdims=True)
+
+    chosen, again = chosen_ref[...], again_ref[...]
+    shape = (npass, stored)
+    entry = jnp.sum(jnp.where(column(chosen, npass, 0) == iota(shape, 1), place_ref[...], 0),
+                    axis=1, keepdims=True)
+    entry_ref[...] = entry
+    shape = (npass, npass)
+    entry_row = jnp.sum(jnp.where(iota(shape, 0) == iota(shape, 1), entry, 0), axis=0,
+                        keepdims=True)
+    in_passage = again // plen == iota((npass, recomputed), 0)
+    at_token = column(again, recomputed, 0) % plen == iota((recomputed, plen), 1)
+    replaced = jnp.dot(jnp.where(in_passage, 1.0, 0.0).astype(jnp.bfloat16),
+                       jnp.where(at_token, 1.0, 0.0).astype(jnp.bfloat16),
+                       preferred_element_type=jnp.float32)
+    live = jnp.where(replaced > 0.5, 0.0, 1.0)
+    live_ref[...] = live
+    index = iota((rows, 1), 0) + mine * rows
+    row_pos = jnp.where(index < recomputed, column(again, rows, mine * rows),
+                        npass * plen + index - recomputed)
+    row_pass = row_pos // plen
+    shape = (rows, npass)
+    within = row_pass == iota(shape, 1)
+    before_ref[...] = jnp.where(iota(shape, 1) < row_pass, 1.0, 0.0).astype(jnp.bfloat16)
+    slot_ref[...] = jnp.sum(jnp.where(within, entry_row + 1, 0), axis=1, keepdims=True) - 1
     edge_ref[...] = jnp.where(
-        token <= offset_ref[...],
-        jnp.dot(within_ref[...], live_ref[...], preferred_element_type=jnp.float32), 0.0)
+        iota((rows, plen), 1) <= row_pos % plen,
+        jnp.dot(jnp.where(within, 1.0, 0.0).astype(jnp.bfloat16), live.astype(jnp.bfloat16),
+                preferred_element_type=jnp.float32), 0.0)
     row = lax.broadcasted_iota(jnp.int32, (rows, 2 * new_half), 0) + mine * rows
     column = lax.broadcasted_iota(jnp.int32, (rows, 2 * new_half), 1)
     new_bias_ref[...] = jnp.where(column <= row, 0.0, MASKED)
@@ -224,45 +254,23 @@
     slots, half_len, kv_local, _, head_dim = cache_kv.shape
     npass = retrieval.shape[1]
     new_rows, heads = new_q.shape[1:3]
-    rc_rows = recompute.shape[1]
     owners = lax.axis_size("cache")
     holders = lax.axis_size("kvsplit")
     half_index = lax.axis_index("kvsplit")
     plen = half_len * holders
-    ctx = npass * plen
     rows = new_rows // holders
 
     own = cache_kv.transpose(2, 3, 0, 1, 4).reshape(kv_local, 2, slots * half_len, head_dim)
     fresh = new_kv[0].transpose(1, 2, 0, 3)
 
-    passages = jnp.arange(passage_slot.shape[0], dtype=jnp.int32)
-    chosen = jnp.sum(
-        jnp.where(retrieval[0][:, None] == passages[None, :], passage_slot[None, :], 0), axis=1
-    )
-    question = ctx + jnp.arange(new_rows - rc_rows, dtype=jnp.int32)
-    row_pos = jnp.concatenate([recompute[0], question])
-    row_pos = lax.dynamic_slice_in_dim(row_pos, half_index * rows, rows, 0)
-    row_pass, row_off = row_pos // plen, row_pos % plen
-    context = jnp.arange(ctx, dtype=jnp.int32)
-    live = jnp.logical_not(jnp.any(context[:, None] == recompute[0][None, :], axis=1))
-    live = live.reshape(npass, holders, half_len).astype(jnp.bfloat16)
-    entry = jnp.arange(npass, dtype=jnp.int32)
-    before = (entry[None, :] < row_pass[:, None]).astype(jnp.bfloat16)
-    within = (entry[None, :] == row_pass[:, None])
-    row_slot = jnp.sum(jnp.where(within, chosen[None, :] + 1, 0), axis=1) - 1
-    slot = jnp.arange(owners * slots, dtype=jnp.int32).reshape(owners, slots)
     keys = holders * slots * half_len
-    held = (chosen[None, :, None] == slot[:, None, :]).astype(jnp.bfloat16)
-    stored = held[:, :, None, :, None] * live[None, :, :, None, :]
-    stored = stored.reshape(owners, npass, keys)
-
     queries = lax.dynamic_slice_in_dim(new_q[0], half_index * rows, rows, 0).transpose(1, 0, 2)
     score_scale = head_dim ** (-0.5) * math.log2(math.e)
     dma = pltpu.SemaphoreType.DMA
     result = pl.pallas_call(
-        functools.partial(kernel, score_scale, 2, owners),
+        functools.partial(kernel, score_scale, 1, owners),
         out_shape=jax.ShapeDtypeStruct((rows, heads * head_dim), jnp.bfloat16),
-        in_specs=[pl.BlockSpec(memory_space=pltpu.VMEM)] * 9,
+        in_specs=[pl.BlockSpec(memory_space=pltpu.VMEM)] * 6,
         out_specs=pl.BlockSpec(memory_space=pltpu.VMEM),
         scratch_shapes=[
             pltpu.VMEM((heads, rows, 2 * head_dim), jnp.float32),
@@ -272,6 +280,10 @@
             pltpu.VMEM((rows, keys), jnp.float32),
             pltpu.VMEM((rows, new_rows), jnp.float32),
             pltpu.VMEM((rows, plen), jnp.float32),
+            pltpu.VMEM((npass, plen), jnp.float32),
+            pltpu.VMEM((rows, npass), jnp.bfloat16),
+            pltpu.VMEM((rows, 1), jnp.int32),
+            pltpu.VMEM((npass, 1), jnp.int32),
             pltpu.VMEM((owners, holders) + own.shape, jnp.bfloat16),
             pltpu.VMEM((holders,) + fresh.shape, jnp.bfloat16),
             dma((2, owners, kv_local)),
@@ -283,8 +295,7 @@
         ],
         compiler_params=pltpu.CompilerParams(
             vmem_limit_bytes=56 * 1024 * 1024, collective_id=0, has_side_effects=True),
-    )(queries, fresh, own, stored, live.reshape(npass, plen), before,
-      within.astype(jnp.bfloat16), row_slot[:, None], row_off[:, None])
+    )(queries, fresh, own, passage_slot[None, :], retrieval, recompute)
     return result[None]
 
 

time: 68.3 us -> 57.6 us (0.84)
  Pallas kernels: 55.1 us -> 50.3 us
  other arithmetic: 4.73 us -> 0 us
  local copies, waits for them, and re-layouts: 8.22 us -> 7.02 us
    pallas_call x1, Pallas kernels: 55.1 us -> 50.3 us  [on_device(): pl.pallas_call(functools.partial(kernel, score_scale, 1, owners), out_sha...]
    reduce_or x1 -> x0, other arithmetic: 1.3 us -> none  [on_device(): jnp.any(context[:, None] == recompute[0][None, :], axis=1)]
    reduce_sum x2 -> x0, other arithmetic: 1.19 us -> none  [the longest x1 1 us: on_device(): jnp.sum(jnp.where(retrieval[0][:, None] == passages[None, :], passage_slo...]
    transpose x1, local copies, waits for them, and re-layouts: 0.9 us -> 1.94 us  [on_device(): cache_kv.transpose(2, 3, 0, 1, 4)]
    convert_element_type x3 -> x0, other arithmetic: 0.8 us -> none  [the longest x1 0.72 us: on_device(): within.astype(jnp.bfloat16)]
    sub x1 -> x0, local copies, waits for them, and re-layouts: 0.77 us -> none  [on_device(): row_slot = jnp.sum(jnp.where(within, chosen[None, :] + 1, 0), axis=1) - 1]
    broadcast_in_dim x1 -> x0, local copies, waits for them, and re-layouts: 0.77 us -> none  [on_device(): row_off[:, None]]
    concatenate x1 -> x0, other arithmetic: 0.69 us -> none  [on_device(): row_pos = jnp.concatenate([recompute[0], question])]
where the time goes in v2:
time: 57.6 us; the launch traced here: 57.3 us
  Pallas kernels  50.3 us (87%)
  local copies, waits for them, and re-layouts  7.02 us (12%)
    pallas_call x1, Pallas kernels, on_device(): pl.pallas_call(functools.partial(kernel, score_scale, 1, owners), out_sha...  50.3 us
    unnamed x4, local copies, waits for them, and re-layouts  3.86 us
    transpose x1, local copies, waits for them, and re-layouts, on_device(): cache_kv.transpose(2, 3, 0, 1, 4)  1.94 us
    dynamic_slice x2, local copies, waits for them, and re-layouts, on_device(): lax.dynamic_slice_in_dim(new_q[0], half_index * rows, rows, 0)  1.22 us

profile of v2, /device:TPU:0, one launch (start us, length us, event | category | flops | bytes accessed | tf_op | source)
XLA Modules:
  0.0 57.3 jit_solution(7440893812569057212)
XLA Ops:
  0.0 0.0 copy-start
  0.0 1.8 %copy.13 = bf16[1,192,2,2,128]{4,1,3,2,0:T(8,128)(2,1)} copy(bf16[1,192,2,2,128]{4,3,2,1,0:T(2,128)(2,1)} %param.11) | data formatting | bytes 393216 | tf_op args[5]
  1.8 1.9 %copy.9 = bf16[2,2,4,128,128]{4,3,2,1,0:T(8,128)(2,1)} copy(bf16[2,2,4,128,128]{4,1,0,3,2:T(2,128)(2,1)} %bitcast.18) | data formatting | bytes 1048576 | tf_op jit(solution)/shard_map/transpose | solution.py:263
  3.7 0.0 copy-done
  3.7 0.1 constant_dynamic-slice_fusion
  3.9 1.1 %copy.12 = bf16[1,192,16,128]{3,1,2,0:T(8,128)(2,1)} copy(bf16[1,192,16,128]{3,2,1,0:T(8,128)(2,1)S(1)} %constant_dynamic-slice_fusion) | data formatting | bytes 1572864 | tf_op jit(solution)/shard_map/dynamic_slice | solution.py:267
  4.9 50.3 %shard_map.64 = bf16[192,2048]{1,0:T(8,128)(2,1)} custom-call(bf16[16,192,128]{2,1,0:T(8,128)(2,1)} %bitcast.14, bf16[2,2,192,128]{3,2,1,0:T(8,128)(2,1)} %bitcast.17, bf16[2,2,512,128]{3,2,1,0:T(8,128)(2,1)} %bitcast.16, s32[1,16]{1,0:T(1,128)} %bitcast.19, s32[1,16]{1,0:T(1,128)} %chosen_ref.1, s32[1,256]{1,0:T(1,128)} %again_ref.1), custom_call_target="tpu_custom_call" | custom-call | tf_op jit(solution)/shard_map/pallas_call | solution.py:270
  55.2 2.1 %copy.15 = bf16[1,192,2048]{2,1,0:T(8,128)(2,1)} copy(bf16[1,192,2048]{2,1,0:T(8,128)(2,1)} %bitcast.15) | data formatting | bytes 1572864
Async XLA Ops:
  0.0 3.7 %copy-start = (bf16[1,384,16,128]{3,2,1,0:T(8,128)(2,1)S(1)}, bf16[1,384,16,128]{3,2,1,0:T(8,128)(2,1)}, u32[]{:S(2)}) copy-start(bf16[1,384,16,128]{3,2,1,0:T(8,128)(2,1)} %param.10) | copy-start | bytes 4718596

commit v3 on v2

--- a/solution.py
+++ b/solution.py
@@ -110,7 +110,11 @@
         left = jnp.where(both, k % 2, jnp.where(z > owners - 1 - z, 0, 1)) == 0
         return jnp.where(left, z - far, z + far), left
 
-    def arrive(k, kv):
+    def arrive(unit):
+        both = unit < 2 * near * kv_local
+        turn = unit % (2 * kv_local)
+        k = jnp.where(both, unit // (2 * kv_local) * 2 + turn % 2, unit // kv_local)
+        kv = jnp.where(both, turn // 2, unit % kv_local)
         owner, left = source(k)
         block = corpus_ref.at[owner, mine, kv]
         side = side_copy(block, owner, kv)
@@ -203,7 +207,7 @@
 
     def turn(k, carry):
         for kv in range(kv_local):
-            arrive(k, kv)
+            arrive(k * kv_local + kv)
             if kv == 0:
                 compute(jnp.where(k == 0, z, source(jnp.maximum(k - 1, 0))[0]), kv_local - 1)
             else:

time: 57.6 us -> 55.6 us (0.965)
  Pallas kernels: 50.3 us -> 48.3 us
    pallas_call x1, Pallas kernels: 50.3 us -> 48.3 us  [on_device(): pl.pallas_call(functools.partial(kernel, score_scale, 1, owners), out_sha...]
where the time goes in v3:
time: 55.6 us; the launch traced here: 55.3 us
  Pallas kernels  48.3 us (87%)
  local copies, waits for them, and re-layouts  7.02 us (13%)
    pallas_call x1, Pallas kernels, on_device(): pl.pallas_call(functools.partial(kernel, score_scale, 1, owners), out_sha...  48.3 us
    unnamed x4, local copies, waits for them, and re-layouts  3.86 us
    transpose x1, local copies, waits for them, and re-layouts, on_device(): cache_kv.transpose(2, 3, 0, 1, 4)  1.94 us
    dynamic_slice x2, local copies, waits for them, and re-layouts, on_device(): lax.dynamic_slice_in_dim(new_q[0], half_index * rows, rows, 0)  1.22 us

profile of v3, /device:TPU:0, one launch (start us, length us, event | category | flops | bytes accessed | tf_op | source)
XLA Modules:
  0.0 55.3 jit_solution(2907856627508825396)
XLA Ops:
  0.0 0.0 copy-start
  0.0 1.8 %copy.13 = bf16[1,192,2,2,128]{4,1,3,2,0:T(8,128)(2,1)} copy(bf16[1,192,2,2,128]{4,3,2,1,0:T(2,128)(2,1)} %param.11) | data formatting | bytes 393216 | tf_op args[5]
  1.8 1.9 %copy.9 = bf16[2,2,4,128,128]{4,3,2,1,0:T(8,128)(2,1)} copy(bf16[2,2,4,128,128]{4,1,0,3,2:T(2,128)(2,1)} %bitcast.18) | data formatting | bytes 1048576 | tf_op jit(solution)/shard_map/transpose | solution.py:267
  3.7 0.0 copy-done
  3.7 0.1 constant_dynamic-slice_fusion
  3.9 1.1 %copy.12 = bf16[1,192,16,128]{3,1,2,0:T(8,128)(2,1)} copy(bf16[1,192,16,128]{3,2,1,0:T(8,128)(2,1)S(1)} %constant_dynamic-slice_fusion) | data formatting | bytes 1572864 | tf_op jit(solution)/shard_map/dynamic_slice | solution.py:271
  4.9 48.3 %shard_map.64 = bf16[192,2048]{1,0:T(8,128)(2,1)} custom-call(bf16[16,192,128]{2,1,0:T(8,128)(2,1)} %bitcast.14, bf16[2,2,192,128]{3,2,1,0:T(8,128)(2,1)} %bitcast.17, bf16[2,2,512,128]{3,2,1,0:T(8,128)(2,1)} %bitcast.16, s32[1,16]{1,0:T(1,128)} %bitcast.19, s32[1,16]{1,0:T(1,128)} %chosen_ref.1, s32[1,256]{1,0:T(1,128)} %again_ref.1), custom_call_target="tpu_custom_call" | custom-call | tf_op jit(solution)/shard_map/pallas_call | solution.py:274
  53.2 2.1 %copy.15 = bf16[1,192,2048]{2,1,0:T(8,128)(2,1)} copy(bf16[1,192,2048]{2,1,0:T(8,128)(2,1)} %bitcast.15) | data formatting | bytes 1572864
Async XLA Ops:
  0.0 3.7 %copy-start = (bf16[1,384,16,128]{3,2,1,0:T(8,128)(2,1)S(1)}, bf16[1,384,16,128]{3,2,1,0:T(8,128)(2,1)}, u32[]{:S(2)}) copy-start(bf16[1,384,16,128]{3,2,1,0:T(8,128)(2,1)} %param.10) | copy-start | bytes 4718596

commit v4 on v3

--- a/solution.py
+++ b/solution.py
@@ -73,10 +73,11 @@
     peers = 1 + jnp.minimum(z, 1) + jnp.minimum(owners - 1 - z, 1)
     pl.semaphore_wait(barrier, peers)
 
-    def line_copy(block, owner, kv, way):
+    def line_copy(block, owner, kv, way, piece):
         return pltpu.make_async_remote_copy(
-            src_ref=block, dst_ref=corpus_ref.at[owner, mine, kv],
-            send_sem=line_send.at[way, owner, kv], recv_sem=line_recv.at[owner, kv],
+            src_ref=block.at[piece], dst_ref=corpus_ref.at[owner, mine, kv, piece],
+            send_sem=line_send.at[way, owner, kv, piece],
+            recv_sem=line_recv.at[owner, kv, piece],
             device_id={"cache": z + 1 if way else z - 1}, device_id_type=MESH)
 
     def side_copy(block, owner, kv):
@@ -92,11 +93,13 @@
     for kv in range(kv_local):
         @pl.when(has_left)
         def _():
-            line_copy(own_ref.at[kv], z, kv, 0).start()
+            for piece in range(2):
+                line_copy(own_ref.at[kv], z, kv, 0, piece).start()
 
         @pl.when(has_right)
         def _():
-            line_copy(own_ref.at[kv], z, kv, 1).start()
+            for piece in range(2):
+                line_copy(own_ref.at[kv], z, kv, 1, piece).start()
 
     new_copy.start()
     for kv in range(kv_local):
@@ -118,15 +121,16 @@
         owner, left = source(k)
         block = corpus_ref.at[owner, mine, kv]
         side = side_copy(block, owner, kv)
-        line_copy(block, owner, kv, 1).wait_recv()
-
-        @pl.when(jnp.logical_and(left, has_right))
-        def _():
-            line_copy(block, owner, kv, 1).start()
-
-        @pl.when(jnp.logical_and(jnp.logical_not(left), has_left))
-        def _():
-            line_copy(block, owner, kv, 0).start()
+        for piece in range(2):
+            line_copy(block, owner, kv, 1, piece).wait_recv()
+
+            @pl.when(jnp.logical_and(left, has_right))
+            def _():
+                line_copy(block, owner, kv, 1, piece).start()
+
+            @pl.when(jnp.logical_and(jnp.logical_not(left), has_left))
+            def _():
+                line_copy(block, owner, kv, 0, piece).start()
 
         side.start()
 
@@ -226,11 +230,13 @@
     for kv in range(kv_local):
         @pl.when(has_left)
         def _():
-            line_copy(own_ref.at[kv], z, kv, 0).wait_send()
+            for piece in range(2):
+                line_copy(own_ref.at[kv], z, kv, 0, piece).wait_send()
 
         @pl.when(has_right)
         def _():
-            line_copy(own_ref.at[kv], z, kv, 1).wait_send()
+            for piece in range(2):
+                line_copy(own_ref.at[kv], z, kv, 1, piece).wait_send()
 
         side_copy(own_ref.at[kv], z, kv).wait_send()
     new_copy.wait_send()
@@ -242,11 +248,13 @@
 
             @pl.when(jnp.logical_and(left, has_right))
             def _():
-                line_copy(block, owner, kv, 1).wait_send()
+                for piece in range(2):
+                    line_copy(block, owner, kv, 1, piece).wait_send()
 
             @pl.when(jnp.logical_and(jnp.logical_not(left), has_left))
             def _():
-                line_copy(block, owner, kv, 0).wait_send()
+                for piece in range(2):
+                    line_copy(block, owner, kv, 0, piece).wait_send()
 
             side_copy(block, owner, kv).wait_send()
         return carry
@@ -290,8 +298,8 @@
             pltpu.VMEM((npass, 1), jnp.int32),
             pltpu.VMEM((owners, holders) + own.shape, jnp.bfloat16),
             pltpu.VMEM((holders,) + fresh.shape, jnp.bfloat16),
-            dma((2, owners, kv_local)),
-            dma((owners, kv_local)),
+            dma((2, owners, kv_local, 2)),
+            dma((owners, kv_local, 2)),
             dma((owners, kv_local)),
             dma((owners, kv_local)),
             dma(()),

time: 55.6 us -> 55.8 us (level)
  no operation moved by 1% of the time
where the time goes in v4:
time: 55.8 us; the launch traced here: 55.6 us
  Pallas kernels  48.6 us (87%)
  local copies, waits for them, and re-layouts  7.02 us (13%)
    pallas_call x1, Pallas kernels, on_device(): pl.pallas_call(functools.partial(kernel, score_scale, 1, owners), out_sha...  48.6 us
    unnamed x4, local copies, waits for them, and re-layouts  3.86 us
    transpose x1, local copies, waits for them, and re-layouts, on_device(): cache_kv.transpose(2, 3, 0, 1, 4)  1.94 us
    dynamic_slice x2, local copies, waits for them, and re-layouts, on_device(): lax.dynamic_slice_in_dim(new_q[0], half_index * rows, rows, 0)  1.22 us

profile of v4, /device:TPU:0, one launch (start us, length us, event | category | flops | bytes accessed | tf_op | source)
XLA Modules:
  0.0 55.6 jit_solution(3958377140033031399)
XLA Ops:
  0.0 0.0 copy-start
  0.0 1.8 %copy.13 = bf16[1,192,2,2,128]{4,1,3,2,0:T(8,128)(2,1)} copy(bf16[1,192,2,2,128]{4,3,2,1,0:T(2,128)(2,1)} %param.11) | data formatting | bytes 393216 | tf_op args[5]
  1.8 1.9 %copy.9 = bf16[2,2,4,128,128]{4,3,2,1,0:T(8,128)(2,1)} copy(bf16[2,2,4,128,128]{4,1,0,3,2:T(2,128)(2,1)} %bitcast.18) | data formatting | bytes 1048576 | tf_op jit(solution)/shard_map/transpose | solution.py:275
  3.7 0.0 copy-done
  3.7 0.1 constant_dynamic-slice_fusion
  3.9 1.1 %copy.12 = bf16[1,192,16,128]{3,1,2,0:T(8,128)(2,1)} copy(bf16[1,192,16,128]{3,2,1,0:T(8,128)(2,1)S(1)} %constant_dynamic-slice_fusion) | data formatting | bytes 1572864 | tf_op jit(solution)/shard_map/dynamic_slice | solution.py:279
  4.9 48.6 %shard_map.64 = bf16[192,2048]{1,0:T(8,128)(2,1)} custom-call(bf16[16,192,128]{2,1,0:T(8,128)(2,1)} %bitcast.14, bf16[2,2,192,128]{3,2,1,0:T(8,128)(2,1)} %bitcast.17, bf16[2,2,512,128]{3,2,1,0:T(8,128)(2,1)} %bitcast.16, s32[1,16]{1,0:T(1,128)} %bitcast.19, s32[1,16]{1,0:T(1,128)} %chosen_ref.1, s32[1,256]{1,0:T(1,128)} %again_ref.1), custom_call_target="tpu_custom_call" | custom-call | tf_op jit(solution)/shard_map/pallas_call | solution.py:282
  53.5 2.1 %copy.15 = bf16[1,192,2048]{2,1,0:T(8,128)(2,1)} copy(bf16[1,192,2048]{2,1,0:T(8,128)(2,1)} %bitcast.15) | data formatting | bytes 1572864
Async XLA Ops:
  0.0 3.7 %copy-start = (bf16[1,384,16,128]{3,2,1,0:T(8,128)(2,1)S(1)}, bf16[1,384,16,128]{3,2,1,0:T(8,128)(2,1)}, u32[]{:S(2)}) copy-start(bf16[1,384,16,128]{3,2,1,0:T(8,128)(2,1)} %param.10) | copy-start | bytes 4718596
